TPU v7x, 32 devices: a whole 2x2x4 slice. The times are simulated.
32 devices in a mesh: row: 8 (over y, x, core), col: 4 (over z).
Axes of the slice: x: 2, y: 2, z: 4, core: 2. Of those that a mesh axis runs over, the one named last changes fastest.
Arguments:
- density: bfloat16 [1024, 1024], P('row', 'col'), as said below
- cotangent: bfloat16 [1024, 1024], P('row', 'col'), may hold values from -6 to 6
- block_pattern: int32 [16, 16], P('row', 'col'), may hold values from 0 to 1, as said below
- filter_pattern: int32 [16, 16], P('row', 'col'), may hold values from 0 to 1, as said below
Outputs:
- purified: bfloat16 [1024, 1024], P('row', 'col')
- gradient: bfloat16 [1024, 1024], P('row', 'col')
Inputs may be any that keep to these rules, and one draw needn't show every extreme that they name: density is symmetric. `block_pattern`: symmetric, with ones on the diagonal. `filter_pattern`: symmetric, with ones on the diagonal.
All inputs are finite; a program needn't handle non-finite values.
Results may differ from a plain program's by a relative error of at most 0.0043.
Values may be sent and summed in bfloat16 or wider, within the bound.
No kernel may reach another device: no remote copies, remote signals or barrier semaphores. Data moves between devices by JAX's collectives and lax.ppermute only.
A program may use at most 64 MiB of HBM per device.

v0:
```python
import jax
import jax.numpy as jnp
from jax import lax
from jax.experimental import pallas as pl
from jax.experimental.pallas import tpu as pltpu
from jax.sharding import PartitionSpec as P

IN_HBM = pl.BlockSpec(memory_space=pltpu.HBM)
IN_VMEM = pl.BlockSpec(memory_space=pltpu.VMEM)
IN_SMEM = pl.BlockSpec(memory_space=pltpu.SMEM)
LIMIT = pltpu.CompilerParams(vmem_limit_bytes=32 * 1024 * 1024)
EARLY = pl.CostEstimate(flops=6_000_000_000, bytes_accessed=0, transcendentals=0)


def dot(a, b):
    return jnp.dot(a, b, preferred_element_type=jnp.float32)


def mask(density, cotangent, block_pattern, filter_pattern):
    height, width = density.shape
    block_size = height // block_pattern.shape[0]

    def kernel(*refs):
        pattern_refs, dense_refs = refs[:2], refs[2:4]
        pair_ref, kept_ref, pattern_held, dense_held, sems = refs[4:]
        copies = []
        for k in range(2):
            copies.append(pltpu.make_async_copy(pattern_refs[k], pattern_held.at[k], sems.at[k]))
            copies.append(pltpu.make_async_copy(dense_refs[k], dense_held.at[k], sems.at[2 + k]))
        for copy in copies:
            copy.start()
        for copy in copies:
            copy.wait()
        lane = lax.broadcasted_iota(jnp.int32, (block_size, width), 1) // block_size
        for k in range(2):
            for i in range(height // block_size):
                rows = pl.ds(i * block_size, block_size)
                kept = jnp.zeros((block_size, width), jnp.float32)
                for j in range(width // block_size):
                    kept = jnp.where(lane == j, pattern_held[k, i, j].astype(jnp.float32), kept)
                kept_ref[k, rows, :] = kept
                pair_ref[k, rows, :] = (dense_held[k, rows, :].astype(jnp.float32) * kept).astype(pair_ref.dtype)

    inputs = (block_pattern, filter_pattern, density, cotangent)
    return pl.pallas_call(
        kernel,
        out_shape=(
            pltpu.VMEM((2, height, width), density.dtype),
            pltpu.VMEM((2, height, width), jnp.float32),
        ),
        in_specs=[IN_HBM] * 4,
        out_specs=(IN_VMEM, IN_VMEM),
        scratch_shapes=[
            pltpu.SMEM((2,) + block_pattern.shape, jnp.int32),
            pltpu.VMEM((2, height, width), density.dtype),
            pltpu.SemaphoreType.DMA((4,)),
        ],
        compiler_params=LIMIT,
        name="mask",
    )(*(pltpu.with_memory_space_constraint(x, pltpu.HBM) for x in inputs))


def settle(block):
    def kernel(block_ref, out_ref):
        out_ref[...] = block_ref[...]

    return pl.pallas_call(
        kernel,
        out_shape=pltpu.VMEM(block.shape, block.dtype),
        in_specs=[IN_VMEM],
        out_specs=IN_VMEM,
        cost_estimate=EARLY,
        compiler_params=LIMIT,
        name="settle",
    )(block)


def flips_of(size):
    flips = []
    while 2 ** len(flips) < size:
        flips.insert(0, 2 ** len(flips))
    return flips


def swap(held, axis_name, size, flips):
    return [
        ([at ^ flip for at in ats], lax.ppermute(blocks, axis_name, [(i, i ^ flip) for i in range(size)]))
        for flip in flips
        for ats, blocks in held
    ]


def double(held, axis_name, size, flips):
    for flip in flips:
        ats = [at for entry in held for at in entry[0]]
        blocks = held[0][1] if len(held) == 1 else jnp.concatenate([entry[1] for entry in held])
        held = held + swap([(ats, blocks)], axis_name, size, [flip])
    return held


def forward(held, axis_name, size, flips):
    held = double(held, axis_name, size, flips[:-2])
    far = swap(held, axis_name, size, flips[-2:-1])
    near = swap(held, axis_name, size, flips[-1:])
    return held + far + near + swap(far, axis_name, size, flips[-1:])


def exchange(pair, axis_name, size):
    flips = flips_of(size)
    held = double([([0], pair[None])], axis_name, size, flips[:-2])
    far = swap(held, axis_name, size, flips[-2:-1])
    near = swap(held, axis_name, size, flips[-1:])
    if far and near:
        (far_pairs, near_pairs) = lax.optimization_barrier((far[0][1], near[0][1]))
        far, near = [(far[0][0], far_pairs)], [(near[0][0], near_pairs)]
    held = held + far + near + swap(far, axis_name, size, flips[-1:])
    return [(at, ((pairs, (k, 0)), (pairs, (k, 1)))) for ats, pairs in held for k, at in enumerate(ats)]


def pieces_of(held, refs):
    for (ats, _), ref in zip(held, refs):
        for k, at in enumerate(ats):
            yield at, ref.at[k]


def part(ref, owner, size):
    return ref.at[pl.ds(pl.multiple_of(owner * size, size), size), :]


def settle(block):
    def kernel(block_ref, out_ref):
        out_ref[...] = block_ref[...]

    return pl.pallas_call(
        kernel,
        out_shape=pltpu.VMEM(block.shape, block.dtype),
        in_specs=[IN_VMEM],
        out_specs=IN_VMEM,
        cost_estimate=EARLY,
        compiler_params=LIMIT,
        name="settle",
    )(block)


def call(kernel, name, here, fixed, helds, cols, out_shape, scratch=(), hint=None):
    arrays = [here, *fixed]
    for held in helds:
        arrays += [blocks for _, blocks in held]
    places = {}
    for entry in (entry for held in cols for entry in held):
        for array, _ in entry[1]:
            if id(array) not in places:
                places[id(array)] = len(arrays)
                arrays.append(array)

    def body(*refs):
        fixed_refs, start, lists = refs[1:1 + len(fixed)], 1 + len(fixed), []
        for held in helds:
            lists.append(refs[start:start + len(held)])
            start += len(held)
        col_refs = [
            [(at, [refs[places[id(array)]].at[k] for array, k in blocks]) for at, blocks in held]
            for held in cols
        ]
        kernel(refs[0], fixed_refs, lists, col_refs, refs[len(arrays):])

    return pl.pallas_call(
        body,
        out_shape=out_shape,
        in_specs=[IN_SMEM] + [IN_VMEM] * (len(arrays) - 1),
        out_specs=jax.tree.map(lambda _: IN_VMEM, out_shape),
        scratch_shapes=scratch,
        cost_estimate=hint,
        compiler_params=LIMIT,
        name=name,
    )(*arrays)


def product(pieces, which, cols_ref, here_col):
    width = cols_ref.shape[-1]
    total = None
    for at, blocks in pieces:
        owner = here_col ^ at
        term = dot(blocks[which][...], part(cols_ref, owner, width)[...])
        total = term if total is None else total + term
    return total


def square_step(here, pair, kept, row_held, pair_held):
    _, height, width = pair.shape
    n_row = sum(len(ats) for ats, _ in row_held)

    def kernel(here_ref, fixed, lists, cols, outs):
        pair_ref, kept_ref = fixed
        both_ref, cols_ref = outs
        for at, block in pieces_of(row_held, lists[0]):
            part(cols_ref, here_ref[0] ^ at, height)[...] = block[...]
        square = product(cols[0], 0, cols_ref, here_ref[1])
        both_ref[0] = (square * kept_ref[1]).astype(both_ref.dtype)
        back = product(cols[0], 1, cols_ref, here_ref[1])
        grad = 3.0 * pair_ref[1].astype(jnp.float32) - 2.0 * back
        both_ref[1] = (grad * kept_ref[1]).astype(both_ref.dtype)

    out = (
        pltpu.VMEM((2, height, width), pair.dtype),
        pltpu.VMEM((n_row * height, width), pair.dtype),
    )
    return call(kernel, "square_step", here, (pair, kept), (row_held,), (pair_held,), out)


def purify_step(here, both, kept, masked_cols, both_held):
    _, height, width = both.shape

    def kernel(here_ref, fixed, lists, cols, outs):
        both_ref, kept_ref, cols_ref = fixed
        purified_ref, back_ref = outs
        cubic = product(cols[0], 0, cols_ref, here_ref[1]) * kept_ref[1]
        purified_ref[...] = (3.0 * both_ref[0].astype(jnp.float32) - 2.0 * cubic).astype(purified_ref.dtype)
        back_ref[...] = product(cols[0], 1, cols_ref, here_ref[1])

    out = (pltpu.VMEM((height, width), both.dtype), pltpu.VMEM((height, width), jnp.float32))
    return call(kernel, "purify_step", here, (both, kept, masked_cols), (), (both_held,), out, hint=EARLY)


def last_step(here, kept, purified, back, late_held, pair_held, both_held):
    height, width = back.shape
    n_row = sum(len(ats) for ats, _ in late_held)

    def kernel(here_ref, fixed, lists, cols, outs):
        kept_ref, purified_ref, back_ref = fixed
        out_ref, gradient_ref, late_cols = outs
        out_ref[...] = purified_ref[...]
        for at, block in pieces_of(late_held, lists[0]):
            for k in range(2):
                part(late_cols.at[k], here_ref[0] ^ at, height)[...] = block[k]
        summed = back_ref[...] + product(cols[0], 0, late_cols.at[0], here_ref[1])
        summed = summed - 2.0 * product(cols[1], 0, late_cols.at[1], here_ref[1])
        gradient_ref[...] = (summed * kept_ref[0]).astype(gradient_ref.dtype)

    out = jax.ShapeDtypeStruct((height, width), purified.dtype)
    scratch = [pltpu.VMEM((2, n_row * height, width), purified.dtype)]
    fixed = (kept, purified, back)
    return call(kernel, "last_step", here, fixed, (late_held,), (pair_held, both_held), (out, out), scratch)


def on_device(n_row, n_col, density, cotangent, block_pattern, filter_pattern):
    here = jnp.stack([lax.axis_index("row"), lax.axis_index("col")]).astype(jnp.int32)
    chip_flips, core_flips = flips_of(n_row)[:-1], flips_of(n_row)[-1:]
    pair, kept = mask(density, cotangent, block_pattern, filter_pattern)

    pair_held = exchange(pair, "col", n_col)
    row_held = forward([([0], pair[:1])], "row", n_row, chip_flips)
    row_held = double(row_held, "row", n_row, core_flips)
    at, ((pairs, _), _) = pair_held[-1]
    pairs = settle(pairs)
    pair_held[-1] = (at, ((pairs, (0, 0)), (pairs, (0, 1))))
    both, masked_cols = square_step(here, pair, kept, row_held, pair_held)

    both_held = exchange(both, "col", n_col)
    late_held = forward([([0], jnp.stack([both[1], pair[1]])[None])], "row", n_row, chip_flips)
    late_held = double(late_held, "row", n_row, core_flips)
    purified, back = purify_step(here, both, kept, masked_cols, both_held)
    return last_step(here, kept, purified, back, late_held, pair_held, both_held)


def solution(mesh):
    placed = (P("row", "col"), P("row", "col"), P("row", "col"), P("row", "col"))

    def local(*arrays):
        return on_device(mesh.shape["row"], mesh.shape["col"], *arrays)

    return jax.shard_map(
        local,
        mesh=mesh,
        in_specs=placed,
        out_specs=(P("row", "col"), P("row", "col")),
        check_vma=False,
    )
```

profile of v0, /device:TPU:0, one launch (start us, length us, event | category | flops | bytes accessed | tf_op | source)
XLA Modules:
  0.0 36.9 jit_solution(16663459372059578627)
XLA Ops:
  0.6 0.9 %mask.1 = (bf16[2,128,256]{2,1,0:T(8,128)(2,1)S(1)}, f32[2,128,256]{2,1,0:T(8,128)S(1)}) custom-call(s32[2,4]{1,0:T(2,128)} %refs_0_.1, s32[2,4]{1,0:T(2,128)} %refs_1_.1, bf16[128,256]{1,0:T(8,128)(2,1)} %refs_2_.1, bf16[128,256]{1,0:T(8,128)(2,1)} %refs_3_.1), custom_call_target="tpu_custom_call" | custom-call | tf_op jit(solution)/shard_map/mask/pallas_call | solution.py:45
  1.6 4.1 %collective-permute-start.4 = (bf16[1,2,128,256]{3,2,1,0:T(8,128)(2,1)S(1)}, bf16[1,2,128,256]{3,2,1,0:T(8,128)(2,1)S(1)}, u32[]{:S(2)}, u32[]{:S(2)}) collective-permute-start(bf16[1,2,128,256]{3,2,1,0:T(8,128)(2,1)S(1)} %bitcast.6), channel_id=1, source_target_pairs={{0,2},{1,3},{2,0},{3,1},{4,6},{5,7},{6,4},{7,5},{8,10},{9,11},{10,... | collective-permute-start | bytes 393224 | tf_op jit(solution)/shard_map/ppermute | solution.py:87
  5.7 1.6 %collective-permute-start.5 = (bf16[1,2,128,256]{3,2,1,0:T(8,128)(2,1)S(1)}, bf16[1,2,128,256]{3,2,1,0:T(8,128)(2,1)S(1)}, u32[]{:S(2)}, u32[]{:S(2)}) collective-permute-start(bf16[1,2,128,256]{3,2,1,0:T(8,128)(2,1)S(1)} %bitcast.7), channel_id=1, source_target_pairs={{0,1},{1,0},{2,3},{3,2},{4,5},{5,4},{6,7},{7,6},{8,9},{9,8},{10,11... | collective-permute-start | bytes 393224 | tf_op jit(solution)/shard_map/ppermute | solution.py:87
  7.3 1.6 %collective-permute-start = (bf16[1,128,256]{2,1,0:T(8,128)(2,1)S(1)}, bf16[1,128,256]{2,1,0:T(8,128)(2,1)S(1)}, u32[]{:S(2)}, u32[]{:S(2)}) collective-permute-start(bf16[1,128,256]{2,1,0:T(8,128)(2,1)S(1)} %get-tuple-element.23.refs_3_), channel_id=1, source_target_pairs={{0,16},{4,20},{8,24},{12,28},{16,0},{20,4},{24,8},{28,12},{1,17},{... | collective-permute-start | bytes 196616 | tf_op jit(solution)/shard_map/ppermute | solution.py:87
  8.9 1.5 %collective-permute-start.1 = (bf16[1,128,256]{2,1,0:T(8,128)(2,1)S(1)}, bf16[1,128,256]{2,1,0:T(8,128)(2,1)S(1)}, u32[]{:S(2)}, u32[]{:S(2)}) collective-permute-start(bf16[1,128,256]{2,1,0:T(8,128)(2,1)S(1)} %get-tuple-element.23.refs_3_), channel_id=1, source_target_pairs={{0,8},{4,12},{8,0},{12,4},{16,24},{20,28},{24,16},{28,20},{1,9},{5... | collective-permute-start | bytes 196616 | tf_op jit(solution)/shard_map/ppermute | solution.py:87
  10.3 1.3 %collective-permute-done.refs_4_ = bf16[1,128,256]{2,1,0:T(8,128)(2,1)S(1)} collective-permute-done((bf16[1,128,256]{2,1,0:T(8,128)(2,1)S(1)}, bf16[1,128,256]{2,1,0:T(8,128)(2,1)S(1)}, u32[]{:S(2)}, u32[]{:S(2)}) %collective-permute-start) | collective-permute-done | bytes 65568 | tf_op jit(solution)/shard_map/ppermute | solution.py:87
  11.6 1.5 %collective-permute-start.2 = (bf16[1,128,256]{2,1,0:T(8,128)(2,1)S(1)}, bf16[1,128,256]{2,1,0:T(8,128)(2,1)S(1)}, u32[]{:S(2)}, u32[]{:S(2)}) collective-permute-start(bf16[1,128,256]{2,1,0:T(8,128)(2,1)S(1)} %collective-permute-done.refs_4_), channel_id=1, source_target_pairs={{0,8},{4,12},{8,0},{12,4},{16,24},{20,28},{24,16},{28,20},{1,9},{5... | collective-permute-start | bytes 196616 | tf_op jit(solution)/shard_map/ppermute | solution.py:87
  13.1 0.6 %collective-permute-start.6 = (bf16[1,2,128,256]{3,2,1,0:T(8,128)(2,1)S(1)}, bf16[1,2,128,256]{3,2,1,0:T(8,128)(2,1)S(1)}, u32[]{:S(2)}, u32[]{:S(2)}) collective-permute-start(bf16[1,2,128,256]{3,2,1,0:T(8,128)(2,1)S(1)} %collective-permute-done.4.refs_9_.refs_10_), channel_id=1, source_target_pairs={{0,1},{1,0},{2,3},{3,2},{4,5},{5,4},{6,7},{7,6},{8,9},{9,8},{10,11... | collective-permute-start | bytes 393224 | tf_op jit(solution)/shard_map/ppermute | solution.py:87
  13.7 0.1 pad_add_fusion.refs_0_
  13.8 2.1 %collective-permute-done.2.refs_6_ = bf16[1,128,256]{2,1,0:T(8,128)(2,1)S(1)} collective-permute-done((bf16[1,128,256]{2,1,0:T(8,128)(2,1)S(1)}, bf16[1,128,256]{2,1,0:T(8,128)(2,1)S(1)}, u32[]{:S(2)}, u32[]{:S(2)}) %collective-permute-start.2) | collective-permute-done | bytes 65568 | tf_op jit(solution)/shard_map/ppermute | solution.py:87
  16.0 2.1 %collective-permute-done.6.block_ref = bf16[1,2,128,256]{3,2,1,0:T(8,128)(2,1)S(1)} collective-permute-done((bf16[1,2,128,256]{3,2,1,0:T(8,128)(2,1)S(1)}, bf16[1,2,128,256]{3,2,1,0:T(8,128)(2,1)S(1)}, u32[]{:S(2)}, u32[]{:S(2)}) %collective-permute-start.6) | collective-permute-done | bytes 131104 | tf_op jit(solution)/shard_map/ppermute | solution.py:87
  18.1 0.9 %square_step.1 = (bf16[2,128,256]{2,1,0:T(8,128)(2,1)S(1)}, bf16[1024,256]{1,0:T(8,128)(2,1)S(1)}) custom-call(s32[2]{0:T(128)S(1)} %pad_add_fusion.refs_0_, bf16[2,128,256]{2,1,0:T(8,128)(2,1)S(1)} %get-tuple-element.13.refs_1_, f32[2,128,256]{2,1,0:T(8,128)S(1)} %get-tuple-element.12.refs_2_.refs_1_, bf16[1,128,256]{2,1,0:T(8,128)(2,1)S(1)} %get-tuple-element.23.refs_3_, ...), custom_call_target="tpu_custom_call" | custom-call | tf_op jit(solution)/shard_map/square_step/pallas_call | solution.py:167
  19.0 1.6 %collective-permute-start.10 = (bf16[1,2,128,256]{3,2,1,0:T(8,128)(2,1)S(1)}, bf16[1,2,128,256]{3,2,1,0:T(8,128)(2,1)S(1)}, u32[]{:S(2)}, u32[]{:S(2)}) collective-permute-start(bf16[1,2,128,256]{3,2,1,0:T(8,128)(2,1)S(1)} %maximum_bitcast_fusion.refs_4_), channel_id=1, source_target_pairs={{0,16},{4,20},{8,24},{12,28},{16,0},{20,4},{24,8},{28,12},{1,17},{... | collective-permute-start | bytes 393224 | tf_op jit(solution)/shard_map/ppermute | solution.py:87
  20.6 1.7 %collective-permute-start.7 = (bf16[1,2,128,256]{3,2,1,0:T(8,128)(2,1)S(1)}, bf16[1,2,128,256]{3,2,1,0:T(8,128)(2,1)S(1)}, u32[]{:S(2)}, u32[]{:S(2)}) collective-permute-start(bf16[1,2,128,256]{3,2,1,0:T(8,128)(2,1)S(1)} %bitcast.10), channel_id=1, source_target_pairs={{0,2},{1,3},{2,0},{3,1},{4,6},{5,7},{6,4},{7,5},{8,10},{9,11},{10,... | collective-permute-start | bytes 393224 | tf_op jit(solution)/shard_map/ppermute | solution.py:87
  22.3 1.7 %collective-permute-start.8 = (bf16[1,2,128,256]{3,2,1,0:T(8,128)(2,1)S(1)}, bf16[1,2,128,256]{3,2,1,0:T(8,128)(2,1)S(1)}, u32[]{:S(2)}, u32[]{:S(2)}) collective-permute-start(bf16[1,2,128,256]{3,2,1,0:T(8,128)(2,1)S(1)} %bitcast.11), channel_id=1, source_target_pairs={{0,1},{1,0},{2,3},{3,2},{4,5},{5,4},{6,7},{7,6},{8,9},{9,8},{10,11... | collective-permute-start | bytes 393224 | tf_op jit(solution)/shard_map/ppermute | solution.py:87
  24.1 1.5 %collective-permute-start.11 = (bf16[1,2,128,256]{3,2,1,0:T(8,128)(2,1)S(1)}, bf16[1,2,128,256]{3,2,1,0:T(8,128)(2,1)S(1)}, u32[]{:S(2)}, u32[]{:S(2)}) collective-permute-start(bf16[1,2,128,256]{3,2,1,0:T(8,128)(2,1)S(1)} %maximum_bitcast_fusion.refs_4_), channel_id=1, source_target_pairs={{0,8},{4,12},{8,0},{12,4},{16,24},{20,28},{24,16},{28,20},{1,9},{5... | collective-permute-start | bytes 393224 | tf_op jit(solution)/shard_map/ppermute | solution.py:87
  25.6 0.5 %collective-permute-start.12 = (bf16[1,2,128,256]{3,2,1,0:T(8,128)(2,1)S(1)}, bf16[1,2,128,256]{3,2,1,0:T(8,128)(2,1)S(1)}, u32[]{:S(2)}, u32[]{:S(2)}) collective-permute-start(bf16[1,2,128,256]{3,2,1,0:T(8,128)(2,1)S(1)} %collective-permute-done.10.refs_5_), channel_id=1, source_target_pairs={{0,8},{4,12},{8,0},{12,4},{16,24},{20,28},{24,16},{28,20},{1,9},{5... | collective-permute-start | bytes 393224 | tf_op jit(solution)/shard_map/ppermute | solution.py:87
  26.1 2.9 %collective-permute-done.7.refs_5_.refs_14_ = bf16[1,2,128,256]{3,2,1,0:T(8,128)(2,1)S(1)} collective-permute-done((bf16[1,2,128,256]{3,2,1,0:T(8,128)(2,1)S(1)}, bf16[1,2,128,256]{3,2,1,0:T(8,128)(2,1)S(1)}, u32[]{:S(2)}, u32[]{:S(2)}) %collective-permute-start.7) | collective-permute-done | bytes 131104 | tf_op jit(solution)/shard_map/ppermute | solution.py:87
  29.0 0.4 %collective-permute-done.8.refs_6_.refs_15_ = bf16[1,2,128,256]{3,2,1,0:T(8,128)(2,1)S(1)} collective-permute-done((bf16[1,2,128,256]{3,2,1,0:T(8,128)(2,1)S(1)}, bf16[1,2,128,256]{3,2,1,0:T(8,128)(2,1)S(1)}, u32[]{:S(2)}, u32[]{:S(2)}) %collective-permute-start.8) | collective-permute-done | bytes 131104 | tf_op jit(solution)/shard_map/ppermute | solution.py:87
  29.4 0.4 collective-permute-start.9
  29.8 0.8 %collective-permute-done.12.refs_7_ = bf16[1,2,128,256]{3,2,1,0:T(8,128)(2,1)S(1)} collective-permute-done((bf16[1,2,128,256]{3,2,1,0:T(8,128)(2,1)S(1)}, bf16[1,2,128,256]{3,2,1,0:T(8,128)(2,1)S(1)}, u32[]{:S(2)}, u32[]{:S(2)}) %collective-permute-start.12) | collective-permute-done | bytes 131104 | tf_op jit(solution)/shard_map/ppermute | solution.py:87
  30.8 3.6 %collective-permute-done.9.refs_7_.refs_16_ = bf16[1,2,128,256]{3,2,1,0:T(8,128)(2,1)S(1)} collective-permute-done((bf16[1,2,128,256]{3,2,1,0:T(8,128)(2,1)S(1)}, bf16[1,2,128,256]{3,2,1,0:T(8,128)(2,1)S(1)}, u32[]{:S(2)}, u32[]{:S(2)}) %collective-permute-start.9) | collective-permute-done | bytes 131104 | tf_op jit(solution)/shard_map/ppermute | solution.py:87
  34.4 0.9 %purify_step.1 = (bf16[128,256]{1,0:T(8,128)(2,1)S(1)}, f32[128,256]{1,0:T(8,128)S(1)}) custom-call(s32[2]{0:T(128)S(1)} %pad_add_fusion.refs_0_, bf16[2,128,256]{2,1,0:T(8,128)(2,1)S(1)} %get-tuple-element.16.refs_1_, f32[2,128,256]{2,1,0:T(8,128)S(1)} %get-tuple-element.12.refs_2_.refs_1_, bf16[1024,256]{1,0:T(8,128)(2,1)S(1)} %get-tuple-element.17.refs_3_, ...), custom_call_target="tpu_custom_call" | custom-call | flops 6000000000 | tf_op jit(solution)/shard_map/purify_step/pallas_call | solution.py:167
  35.3 1.6 %last_step.1 = (bf16[128,256]{1,0:T(8,128)(2,1)}, bf16[128,256]{1,0:T(8,128)(2,1)}) custom-call(s32[2]{0:T(128)S(1)} %pad_add_fusion.refs_0_, f32[2,128,256]{2,1,0:T(8,128)S(1)} %get-tuple-element.12.refs_2_.refs_1_, bf16[128,256]{1,0:T(8,128)(2,1)S(1)} %get-tuple-element.20.refs_2_, f32[128,256]{1,0:T(8,128)S(1)} %get-tuple-element.21.refs_3_, ...), custom_call_target="tpu_custom_call" | custom-call | tf_op jit(solution)/shard_map/last_step/pallas_call | solution.py:167
  (15 shorter events, 0.3 us)
Async XLA Ops:
  1.6 11.5 %collective-permute-start.4 = (bf16[1,2,128,256]{3,2,1,0:T(8,128)(2,1)S(1)}, bf16[1,2,128,256]{3,2,1,0:T(8,128)(2,1)S(1)}, u32[]{:S(2)}, u32[]{:S(2)}) collective-permute-start(bf16[1,2,128,256]{3,2,1,0:T(8,128)(2,1)S(1)} %bitcast.6), channel_id=1, source_target_pairs={{0,2},{1,3},{2,0},{3,1},{4,6},{5,7},{6,4},{7,5},{8,10},{9,11},{10,... | collective-permute-start | bytes 393224 | tf_op jit(solution)/shard_map/ppermute | solution.py:87
  5.7 7.4 %collective-permute-start.5 = (bf16[1,2,128,256]{3,2,1,0:T(8,128)(2,1)S(1)}, bf16[1,2,128,256]{3,2,1,0:T(8,128)(2,1)S(1)}, u32[]{:S(2)}, u32[]{:S(2)}) collective-permute-start(bf16[1,2,128,256]{3,2,1,0:T(8,128)(2,1)S(1)} %bitcast.7), channel_id=1, source_target_pairs={{0,1},{1,0},{2,3},{3,2},{4,5},{5,4},{6,7},{7,6},{8,9},{9,8},{10,11... | collective-permute-start | bytes 393224 | tf_op jit(solution)/shard_map/ppermute | solution.py:87
  7.3 4.3 %collective-permute-start = (bf16[1,128,256]{2,1,0:T(8,128)(2,1)S(1)}, bf16[1,128,256]{2,1,0:T(8,128)(2,1)S(1)}, u32[]{:S(2)}, u32[]{:S(2)}) collective-permute-start(bf16[1,128,256]{2,1,0:T(8,128)(2,1)S(1)} %get-tuple-element.23.refs_3_), channel_id=1, source_target_pairs={{0,16},{4,20},{8,24},{12,28},{16,0},{20,4},{24,8},{28,12},{1,17},{... | collective-permute-start | bytes 196616 | tf_op jit(solution)/shard_map/ppermute | solution.py:87
  8.9 5.0 %collective-permute-start.1 = (bf16[1,128,256]{2,1,0:T(8,128)(2,1)S(1)}, bf16[1,128,256]{2,1,0:T(8,128)(2,1)S(1)}, u32[]{:S(2)}, u32[]{:S(2)}) collective-permute-start(bf16[1,128,256]{2,1,0:T(8,128)(2,1)S(1)} %get-tuple-element.23.refs_3_), channel_id=1, source_target_pairs={{0,8},{4,12},{8,0},{12,4},{16,24},{20,28},{24,16},{28,20},{1,9},{5... | collective-permute-start | bytes 196616 | tf_op jit(solution)/shard_map/ppermute | solution.py:87
  11.6 4.3 %collective-permute-start.2 = (bf16[1,128,256]{2,1,0:T(8,128)(2,1)S(1)}, bf16[1,128,256]{2,1,0:T(8,128)(2,1)S(1)}, u32[]{:S(2)}, u32[]{:S(2)}) collective-permute-start(bf16[1,128,256]{2,1,0:T(8,128)(2,1)S(1)} %collective-permute-done.refs_4_), channel_id=1, source_target_pairs={{0,8},{4,12},{8,0},{12,4},{16,24},{20,28},{24,16},{28,20},{1,9},{5... | collective-permute-start | bytes 196616 | tf_op jit(solution)/shard_map/ppermute | solution.py:87
  13.1 5.0 %collective-permute-start.6 = (bf16[1,2,128,256]{3,2,1,0:T(8,128)(2,1)S(1)}, bf16[1,2,128,256]{3,2,1,0:T(8,128)(2,1)S(1)}, u32[]{:S(2)}, u32[]{:S(2)}) collective-permute-start(bf16[1,2,128,256]{3,2,1,0:T(8,128)(2,1)S(1)} %collective-permute-done.4.refs_9_.refs_10_), channel_id=1, source_target_pairs={{0,1},{1,0},{2,3},{3,2},{4,5},{5,4},{6,7},{7,6},{8,9},{9,8},{10,11... | collective-permute-start | bytes 393224 | tf_op jit(solution)/shard_map/ppermute | solution.py:87
  15.9 2.2 %collective-permute-start.3 = (bf16[4,128,256]{2,1,0:T(8,128)(2,1)S(1)}, bf16[4,128,256]{2,1,0:T(8,128)(2,1)S(1)}, u32[]{:S(2)}, u32[]{:S(2)}) collective-permute-start(bf16[4,128,256]{2,1,0:T(8,128)(2,1)S(1)} %pad_maximum_fusion.1), channel_id=1, source_target_pairs={{0,4},{4,0},{8,12},{12,8},{16,20},{20,16},{24,28},{28,24},{1,5},{5... | collective-permute-start | bytes 786440 | tf_op jit(solution)/shard_map/ppermute | solution.py:87
  19.0 6.5 %collective-permute-start.10 = (bf16[1,2,128,256]{3,2,1,0:T(8,128)(2,1)S(1)}, bf16[1,2,128,256]{3,2,1,0:T(8,128)(2,1)S(1)}, u32[]{:S(2)}, u32[]{:S(2)}) collective-permute-start(bf16[1,2,128,256]{3,2,1,0:T(8,128)(2,1)S(1)} %maximum_bitcast_fusion.refs_4_), channel_id=1, source_target_pairs={{0,16},{4,20},{8,24},{12,28},{16,0},{20,4},{24,8},{28,12},{1,17},{... | collective-permute-start | bytes 393224 | tf_op jit(solution)/shard_map/ppermute | solution.py:87
  20.6 8.4 %collective-permute-start.7 = (bf16[1,2,128,256]{3,2,1,0:T(8,128)(2,1)S(1)}, bf16[1,2,128,256]{3,2,1,0:T(8,128)(2,1)S(1)}, u32[]{:S(2)}, u32[]{:S(2)}) collective-permute-start(bf16[1,2,128,256]{3,2,1,0:T(8,128)(2,1)S(1)} %bitcast.10), channel_id=1, source_target_pairs={{0,2},{1,3},{2,0},{3,1},{4,6},{5,7},{6,4},{7,5},{8,10},{9,11},{10,... | collective-permute-start | bytes 393224 | tf_op jit(solution)/shard_map/ppermute | solution.py:87
  22.3 7.1 %collective-permute-start.8 = (bf16[1,2,128,256]{3,2,1,0:T(8,128)(2,1)S(1)}, bf16[1,2,128,256]{3,2,1,0:T(8,128)(2,1)S(1)}, u32[]{:S(2)}, u32[]{:S(2)}) collective-permute-start(bf16[1,2,128,256]{3,2,1,0:T(8,128)(2,1)S(1)} %bitcast.11), channel_id=1, source_target_pairs={{0,1},{1,0},{2,3},{3,2},{4,5},{5,4},{6,7},{7,6},{8,9},{9,8},{10,11... | collective-permute-start | bytes 393224 | tf_op jit(solution)/shard_map/ppermute | solution.py:87
  24.1 5.7 %collective-permute-start.11 = (bf16[1,2,128,256]{3,2,1,0:T(8,128)(2,1)S(1)}, bf16[1,2,128,256]{3,2,1,0:T(8,128)(2,1)S(1)}, u32[]{:S(2)}, u32[]{:S(2)}) collective-permute-start(bf16[1,2,128,256]{3,2,1,0:T(8,128)(2,1)S(1)} %maximum_bitcast_fusion.refs_4_), channel_id=1, source_target_pairs={{0,8},{4,12},{8,0},{12,4},{16,24},{20,28},{24,16},{28,20},{1,9},{5... | collective-permute-start | bytes 393224 | tf_op jit(solution)/shard_map/ppermute | solution.py:87
  25.6 5.0 %collective-permute-start.12 = (bf16[1,2,128,256]{3,2,1,0:T(8,128)(2,1)S(1)}, bf16[1,2,128,256]{3,2,1,0:T(8,128)(2,1)S(1)}, u32[]{:S(2)}, u32[]{:S(2)}) collective-permute-start(bf16[1,2,128,256]{3,2,1,0:T(8,128)(2,1)S(1)} %collective-permute-done.10.refs_5_), channel_id=1, source_target_pairs={{0,8},{4,12},{8,0},{12,4},{16,24},{20,28},{24,16},{28,20},{1,9},{5... | collective-permute-start | bytes 393224 | tf_op jit(solution)/shard_map/ppermute | solution.py:87
  29.4 5.0 %collective-permute-start.9 = (bf16[1,2,128,256]{3,2,1,0:T(8,128)(2,1)S(1)}, bf16[1,2,128,256]{3,2,1,0:T(8,128)(2,1)S(1)}, u32[]{:S(2)}, u32[]{:S(2)}) collective-permute-start(bf16[1,2,128,256]{3,2,1,0:T(8,128)(2,1)S(1)} %collective-permute-done.7.refs_5_.refs_14_), channel_id=1, source_target_pairs={{0,1},{1,0},{2,3},{3,2},{4,5},{5,4},{6,7},{7,6},{8,9},{9,8},{10,11... | collective-permute-start | bytes 393224 | tf_op jit(solution)/shard_map/ppermute | solution.py:87
  30.7 4.6 %collective-permute-start.13 = (bf16[4,2,128,256]{3,2,1,0:T(8,128)(2,1)S(1)}, bf16[4,2,128,256]{3,2,1,0:T(8,128)(2,1)S(1)}, u32[]{:S(2)}, u32[]{:S(2)}) collective-permute-start(bf16[4,2,128,256]{3,2,1,0:T(8,128)(2,1)S(1)} %pad_maximum_fusion), channel_id=1, source_target_pairs={{0,4},{4,0},{8,12},{12,8},{16,20},{20,16},{24,28},{28,24},{1,5},{5... | collective-permute-start | bytes 1572872 | tf_op jit(solution)/shard_map/ppermute | solution.py:87
where the time goes:
time: 37 us; the launch traced here: 36.9 us
  starting transfers between devices  18.4 us (50%)
  waiting for transfers between devices  13.2 us (36%)
  Pallas kernels  4.29 us (12%)
  between operations  0.73 us (2%)
    ppermute x14, starting transfers between devices, swap(): lax.ppermute(blocks, axis_name, [(i, i ^ flip) for i in range(size)])  18.4 us
    ppermute x14, waiting for transfers between devices, swap(): lax.ppermute(blocks, axis_name, [(i, i ^ flip) for i in range(size)])  13.2 us
    pallas_call x3, Pallas kernels, call(): pl.pallas_call(body, out_shape=out_shape, in_specs=[IN_SMEM] + [IN_VMEM]...  3.35 us
    pallas_call x1, Pallas kernels, mask(): pl.pallas_call(kernel, out_shape=(pltpu.VMEM((2, height, width), density....  0.94 us
  transfers between devices with their start and end apart: 14, of which 7 were waited for; matrix products, arithmetic and copies ran while one was open for 1% of the time, Pallas kernels for 2%

commit v1 on v0

--- a/solution.py
+++ b/solution.py
@@ -105,16 +105,23 @@
     return held + far + near + swap(far, axis_name, size, flips[-1:])
 
 
-def exchange(pair, axis_name, size):
-    flips = flips_of(size)
-    held = double([([0], pair[None])], axis_name, size, flips[:-2])
-    far = swap(held, axis_name, size, flips[-2:-1])
-    near = swap(held, axis_name, size, flips[-1:])
-    if far and near:
-        (far_pairs, near_pairs) = lax.optimization_barrier((far[0][1], near[0][1]))
-        far, near = [(far[0][0], far_pairs)], [(near[0][0], near_pairs)]
-    held = held + far + near + swap(far, axis_name, size, flips[-1:])
-    return [(at, ((pairs, (k, 0)), (pairs, (k, 1)))) for ats, pairs in held for k, at in enumerate(ats)]
+def tie(helds):
+    arrays = lax.optimization_barrier([[blocks for _, blocks in held] for held in helds])
+    return [[(ats, block) for (ats, _), block in zip(held, blocks)] for held, blocks in zip(helds, arrays)]
+
+
+def exchange(pair, block, n_row, n_col, later=()):
+    col_flips, row_flips = flips_of(n_col), flips_of(n_row)
+    pairs = double([([0], pair[None])], "col", n_col, col_flips[:-2])
+    blocks = [([0], block)]
+    far = swap(pairs, "col", n_col, col_flips[-2:-1])
+    near = swap(pairs, "col", n_col, col_flips[-1:])
+    first = swap(blocks, "row", n_row, row_flips[:1])
+    far, near, first, later = tie([far, near, first, later])
+    blocks = double(blocks + first, "row", n_row, row_flips[1:])
+    pairs = pairs + far + near + swap(far, "col", n_col, col_flips[-1:])
+    places = [(at, ((array, (k, 0)), (array, (k, 1)))) for ats, array in pairs for k, at in enumerate(ats)]
+    return places, blocks, later
 
 
 def pieces_of(held, refs):
@@ -186,18 +193,23 @@
     return total
 
 
+def fill(cols_ref, held, refs, here_row):
+    height = held[0][1].shape[-2]
+    for at, block in pieces_of(held, refs):
+        part(cols_ref, here_row ^ at, height)[...] = block[...]
+
+
 def square_step(here, pair, kept, row_held, pair_held):
     _, height, width = pair.shape
     n_row = sum(len(ats) for ats, _ in row_held)
 
     def kernel(here_ref, fixed, lists, cols, outs):
         pair_ref, kept_ref = fixed
-        both_ref, cols_ref = outs
-        for at, block in pieces_of(row_held, lists[0]):
-            part(cols_ref, here_ref[0] ^ at, height)[...] = block[...]
-        square = product(cols[0], 0, cols_ref, here_ref[1])
+        both_ref, masked_ref = outs
+        fill(masked_ref, row_held, lists[0], here_ref[0])
+        square = product(cols[0], 0, masked_ref, here_ref[1])
         both_ref[0] = (square * kept_ref[1]).astype(both_ref.dtype)
-        back = product(cols[0], 1, cols_ref, here_ref[1])
+        back = product(cols[0], 1, masked_ref, here_ref[1])
         grad = 3.0 * pair_ref[1].astype(jnp.float32) - 2.0 * back
         both_ref[1] = (grad * kept_ref[1]).astype(both_ref.dtype)
 
@@ -208,59 +220,59 @@
     return call(kernel, "square_step", here, (pair, kept), (row_held,), (pair_held,), out)
 
 
-def purify_step(here, both, kept, masked_cols, both_held):
+def purify_step(here, both, kept, masked_cols, filtered_held, both_held):
     _, height, width = both.shape
 
     def kernel(here_ref, fixed, lists, cols, outs):
-        both_ref, kept_ref, cols_ref = fixed
-        purified_ref, back_ref = outs
-        cubic = product(cols[0], 0, cols_ref, here_ref[1]) * kept_ref[1]
+        both_ref, kept_ref, masked_ref = fixed
+        purified_ref, total_ref, filtered_cols = outs
+        fill(filtered_cols, filtered_held, lists[0], here_ref[0])
+        cubic = product(cols[0], 0, masked_ref, here_ref[1]) * kept_ref[1]
         purified_ref[...] = (3.0 * both_ref[0].astype(jnp.float32) - 2.0 * cubic).astype(purified_ref.dtype)
-        back_ref[...] = product(cols[0], 1, cols_ref, here_ref[1])
+        total = product(cols[0], 1, masked_ref, here_ref[1])
+        total_ref[...] = total - 2.0 * product(cols[0], 0, filtered_cols, here_ref[1])
 
     out = (pltpu.VMEM((height, width), both.dtype), pltpu.VMEM((height, width), jnp.float32))
-    return call(kernel, "purify_step", here, (both, kept, masked_cols), (), (both_held,), out, hint=EARLY)
-
-
-def last_step(here, kept, purified, back, late_held, pair_held, both_held):
-    height, width = back.shape
-    n_row = sum(len(ats) for ats, _ in late_held)
+    scratch = [pltpu.VMEM(masked_cols.shape, masked_cols.dtype)]
+    fixed = (both, kept, masked_cols)
+    return call(kernel, "purify_step", here, fixed, (filtered_held,), (both_held,), out, scratch, hint=EARLY)
+
+
+def last_step(here, kept, purified, total, row_held, pair_held):
+    height, width = total.shape
+    n_row = sum(len(ats) for ats, _ in row_held)
 
     def kernel(here_ref, fixed, lists, cols, outs):
-        kept_ref, purified_ref, back_ref = fixed
-        out_ref, gradient_ref, late_cols = outs
+        kept_ref, purified_ref, total_ref = fixed
+        out_ref, gradient_ref, grad_cols = outs
         out_ref[...] = purified_ref[...]
-        for at, block in pieces_of(late_held, lists[0]):
-            for k in range(2):
-                part(late_cols.at[k], here_ref[0] ^ at, height)[...] = block[k]
-        summed = back_ref[...] + product(cols[0], 0, late_cols.at[0], here_ref[1])
-        summed = summed - 2.0 * product(cols[1], 0, late_cols.at[1], here_ref[1])
+        fill(grad_cols, row_held, lists[0], here_ref[0])
+        summed = total_ref[...] + product(cols[0], 0, grad_cols, here_ref[1])
         gradient_ref[...] = (summed * kept_ref[0]).astype(gradient_ref.dtype)
 
     out = jax.ShapeDtypeStruct((height, width), purified.dtype)
-    scratch = [pltpu.VMEM((2, n_row * height, width), purified.dtype)]
-    fixed = (kept, purified, back)
-    return call(kernel, "last_step", here, fixed, (late_held,), (pair_held, both_held), (out, out), scratch)
+    scratch = [pltpu.VMEM((n_row * height, width), purified.dtype)]
+    fixed = (kept, purified, total)
+    return call(kernel, "last_step", here, fixed, (row_held,), (pair_held,), (out, out), scratch)
 
 
 def on_device(n_row, n_col, density, cotangent, block_pattern, filter_pattern):
     here = jnp.stack([lax.axis_index("row"), lax.axis_index("col")]).astype(jnp.int32)
-    chip_flips, core_flips = flips_of(n_row)[:-1], flips_of(n_row)[-1:]
     pair, kept = mask(density, cotangent, block_pattern, filter_pattern)
 
-    pair_held = exchange(pair, "col", n_col)
-    row_held = forward([([0], pair[:1])], "row", n_row, chip_flips)
-    row_held = double(row_held, "row", n_row, core_flips)
+    pair_held, row_held, filtered = exchange(pair, pair[:1], n_row, n_col, [([0], pair[1:])])
     at, ((pairs, _), _) = pair_held[-1]
     pairs = settle(pairs)
     pair_held[-1] = (at, ((pairs, (0, 0)), (pairs, (0, 1))))
     both, masked_cols = square_step(here, pair, kept, row_held, pair_held)
 
-    both_held = exchange(both, "col", n_col)
-    late_held = forward([([0], jnp.stack([both[1], pair[1]])[None])], "row", n_row, chip_flips)
-    late_held = double(late_held, "row", n_row, core_flips)
-    purified, back = purify_step(here, both, kept, masked_cols, both_held)
-    return last_step(here, kept, purified, back, late_held, pair_held, both_held)
+    filtered_held = double(filtered, "row", n_row, flips_of(n_row))
+    both_held, grad_held, _ = exchange(both, both[1:], n_row, n_col)
+    at, ((pairs, _), _) = both_held[-1]
+    pairs = settle(pairs)
+    both_held[-1] = (at, ((pairs, (0, 0)), (pairs, (0, 1))))
+    purified, total = purify_step(here, both, kept, masked_cols, filtered_held, both_held)
+    return last_step(here, kept, purified, total, grad_held, pair_held)
 
 
 def solution(mesh):

time: 37 us -> 38.6 us (1.043)
  starting transfers between devices: 18.4 us -> 21.2 us
  waiting for transfers between devices: 13.2 us -> 12 us
    ppermute x14 -> x15, starting transfers between devices: 18.4 us -> 21.2 us  [swap(): lax.ppermute(blocks, axis_name, [(i, i ^ flip) for i in range(size)])]
    ppermute x14 -> x15, waiting for transfers between devices: 13.2 us -> 12 us  [swap(): lax.ppermute(blocks, axis_name, [(i, i ^ flip) for i in range(size)])]
  transfers between devices with their start and end apart: 14 -> 15, of which waited for: 7 -> 11; matrix products, arithmetic and copies ran while one was open for 1% -> 1% of each run, Pallas kernels for 2% -> 5%
where the time goes in v1:
time: 38.6 us; the launch traced here: 38.4 us
  starting transfers between devices  21.2 us (55%)
  waiting for transfers between devices  12 us (31%)
  Pallas kernels  4.27 us (11%)
  between operations  0.74 us (2%)
    ppermute x15, starting transfers between devices, swap(): lax.ppermute(blocks, axis_name, [(i, i ^ flip) for i in range(size)])  21.2 us
    ppermute x15, waiting for transfers between devices, swap(): lax.ppermute(blocks, axis_name, [(i, i ^ flip) for i in range(size)])  12 us
    pallas_call x3, Pallas kernels, call(): pl.pallas_call(body, out_shape=out_shape, in_specs=[IN_SMEM] + [IN_VMEM]...  3.31 us
    pallas_call x1, Pallas kernels, mask(): pl.pallas_call(kernel, out_shape=(pltpu.VMEM((2, height, width), density....  0.94 us
  transfers between devices with their start and end apart: 15, of which 11 were waited for; matrix products, arithmetic and copies ran while one was open for 1% of the time, Pallas kernels for 5%

profile of v1, /device:TPU:0, one launch (start us, length us, event | category | flops | bytes accessed | tf_op | source)
XLA Modules:
  0.0 38.4 jit_solution(15380606376679393913)
XLA Ops:
  0.6 0.9 %mask.1 = (bf16[2,128,256]{2,1,0:T(8,128)(2,1)S(1)}, f32[2,128,256]{2,1,0:T(8,128)S(1)}) custom-call(s32[2,4]{1,0:T(2,128)} %refs_0_.1, s32[2,4]{1,0:T(2,128)} %refs_1_.1, bf16[128,256]{1,0:T(8,128)(2,1)} %refs_2_.1, bf16[128,256]{1,0:T(8,128)(2,1)} %refs_3_.1), custom_call_target="tpu_custom_call" | custom-call | tf_op jit(solution)/shard_map/mask/pallas_call | solution.py:45
  1.6 4.1 %collective-permute-start = (bf16[1,2,128,256]{3,2,1,0:T(8,128)(2,1)S(1)}, bf16[1,2,128,256]{3,2,1,0:T(8,128)(2,1)S(1)}, u32[]{:S(2)}, u32[]{:S(2)}) collective-permute-start(bf16[1,2,128,256]{3,2,1,0:T(8,128)(2,1)S(1)} %bitcast.4), channel_id=1, source_target_pairs={{0,2},{1,3},{2,0},{3,1},{4,6},{5,7},{6,4},{7,5},{8,10},{9,11},{10,... | collective-permute-start | bytes 393224 | tf_op jit(solution)/shard_map/ppermute | solution.py:87
  5.7 1.6 %collective-permute-start.1 = (bf16[1,2,128,256]{3,2,1,0:T(8,128)(2,1)S(1)}, bf16[1,2,128,256]{3,2,1,0:T(8,128)(2,1)S(1)}, u32[]{:S(2)}, u32[]{:S(2)}) collective-permute-start(bf16[1,2,128,256]{3,2,1,0:T(8,128)(2,1)S(1)} %bitcast.5), channel_id=1, source_target_pairs={{0,1},{1,0},{2,3},{3,2},{4,5},{5,4},{6,7},{7,6},{8,9},{9,8},{10,11... | collective-permute-start | bytes 393224 | tf_op jit(solution)/shard_map/ppermute | solution.py:87
  7.3 1.6 %collective-permute-start.2 = (bf16[1,128,256]{2,1,0:T(8,128)(2,1)S(1)}, bf16[1,128,256]{2,1,0:T(8,128)(2,1)S(1)}, u32[]{:S(2)}, u32[]{:S(2)}) collective-permute-start(bf16[1,128,256]{2,1,0:T(8,128)(2,1)S(1)} %get-tuple-element.29.refs_3_), channel_id=1, source_target_pairs={{0,16},{4,20},{8,24},{12,28},{16,0},{20,4},{24,8},{28,12},{1,17},{... | collective-permute-start | bytes 196616 | tf_op jit(solution)/shard_map/ppermute | solution.py:87
  8.9 2.7 %collective-permute-done.2.refs_4_ = bf16[1,128,256]{2,1,0:T(8,128)(2,1)S(1)} collective-permute-done((bf16[1,128,256]{2,1,0:T(8,128)(2,1)S(1)}, bf16[1,128,256]{2,1,0:T(8,128)(2,1)S(1)}, u32[]{:S(2)}, u32[]{:S(2)}) %collective-permute-start.2) | collective-permute-done | bytes 65568 | tf_op jit(solution)/shard_map/ppermute | solution.py:87
  11.6 0.5 %collective-permute-done.refs_8_.refs_9_ = bf16[1,2,128,256]{3,2,1,0:T(8,128)(2,1)S(1)} collective-permute-done((bf16[1,2,128,256]{3,2,1,0:T(8,128)(2,1)S(1)}, bf16[1,2,128,256]{3,2,1,0:T(8,128)(2,1)S(1)}, u32[]{:S(2)}, u32[]{:S(2)}) %collective-permute-start) | collective-permute-done | bytes 131104 | tf_op jit(solution)/shard_map/ppermute | solution.py:87
  12.3 1.6 %collective-permute-start.3 = (bf16[2,128,256]{2,1,0:T(8,128)(2,1)S(1)}, bf16[2,128,256]{2,1,0:T(8,128)(2,1)S(1)}, u32[]{:S(2)}, u32[]{:S(2)}) collective-permute-start(bf16[2,128,256]{2,1,0:T(8,128)(2,1)S(1)} %pad_maximum_fusion.3), channel_id=1, source_target_pairs={{0,8},{4,12},{8,0},{12,4},{16,24},{20,28},{24,16},{28,20},{1,9},{5... | collective-permute-start | bytes 393224 | tf_op jit(solution)/shard_map/ppermute | solution.py:87
  13.9 1.4 %collective-permute-start.5 = (bf16[1,2,128,256]{3,2,1,0:T(8,128)(2,1)S(1)}, bf16[1,2,128,256]{3,2,1,0:T(8,128)(2,1)S(1)}, u32[]{:S(2)}, u32[]{:S(2)}) collective-permute-start(bf16[1,2,128,256]{3,2,1,0:T(8,128)(2,1)S(1)} %collective-permute-done.refs_8_.refs_9_), channel_id=1, source_target_pairs={{0,1},{1,0},{2,3},{3,2},{4,5},{5,4},{6,7},{7,6},{8,9},{9,8},{10,11... | collective-permute-start | bytes 393224 | tf_op jit(solution)/shard_map/ppermute | solution.py:87
  15.4 1.5 %collective-permute-start.6 = (bf16[1,128,256]{2,1,0:T(8,128)(2,1)S(1)}, bf16[1,128,256]{2,1,0:T(8,128)(2,1)S(1)}, u32[]{:S(2)}, u32[]{:S(2)}) collective-permute-start(bf16[1,128,256]{2,1,0:T(8,128)(2,1)S(1)} %get-tuple-element.22.refs_4_), channel_id=1, source_target_pairs={{0,16},{4,20},{8,24},{12,28},{16,0},{20,4},{24,8},{28,12},{1,17},{... | collective-permute-start | bytes 196616 | tf_op jit(solution)/shard_map/ppermute | solution.py:87
  16.9 0.4 %collective-permute-done.3.refs_5_ = bf16[2,128,256]{2,1,0:T(8,128)(2,1)S(1)} collective-permute-done((bf16[2,128,256]{2,1,0:T(8,128)(2,1)S(1)}, bf16[2,128,256]{2,1,0:T(8,128)(2,1)S(1)}, u32[]{:S(2)}, u32[]{:S(2)}) %collective-permute-start.3) | collective-permute-done | bytes 131104 | tf_op jit(solution)/shard_map/ppermute | solution.py:87
  17.5 1.4 %collective-permute-done.5.block_ref = bf16[1,2,128,256]{3,2,1,0:T(8,128)(2,1)S(1)} collective-permute-done((bf16[1,2,128,256]{3,2,1,0:T(8,128)(2,1)S(1)}, bf16[1,2,128,256]{3,2,1,0:T(8,128)(2,1)S(1)}, u32[]{:S(2)}, u32[]{:S(2)}) %collective-permute-start.5) | collective-permute-done | bytes 131104 | tf_op jit(solution)/shard_map/ppermute | solution.py:87
  19.0 0.9 %square_step.1 = (bf16[2,128,256]{2,1,0:T(8,128)(2,1)S(1)}, bf16[1024,256]{1,0:T(8,128)(2,1)S(1)}) custom-call(s32[2]{0:T(128)S(1)} %pad_add_fusion.refs_0_, bf16[2,128,256]{2,1,0:T(8,128)(2,1)S(1)} %get-tuple-element.16.refs_1_, f32[2,128,256]{2,1,0:T(8,128)S(1)} %get-tuple-element.15.refs_2_.refs_1_, bf16[1,128,256]{2,1,0:T(8,128)(2,1)S(1)} %get-tuple-element.29.refs_3_, ...), custom_call_target="tpu_custom_call" | custom-call | tf_op jit(solution)/shard_map/square_step/pallas_call | solution.py:174
  19.9 2.2 %collective-permute-start.9 = (bf16[1,2,128,256]{3,2,1,0:T(8,128)(2,1)S(1)}, bf16[1,2,128,256]{3,2,1,0:T(8,128)(2,1)S(1)}, u32[]{:S(2)}, u32[]{:S(2)}) collective-permute-start(bf16[1,2,128,256]{3,2,1,0:T(8,128)(2,1)S(1)} %bitcast.8), channel_id=1, source_target_pairs={{0,2},{1,3},{2,0},{3,1},{4,6},{5,7},{6,4},{7,5},{8,10},{9,11},{10,... | collective-permute-start | bytes 393224 | tf_op jit(solution)/shard_map/ppermute | solution.py:87
  22.1 2.1 %collective-permute-start.10 = (bf16[1,2,128,256]{3,2,1,0:T(8,128)(2,1)S(1)}, bf16[1,2,128,256]{3,2,1,0:T(8,128)(2,1)S(1)}, u32[]{:S(2)}, u32[]{:S(2)}) collective-permute-start(bf16[1,2,128,256]{3,2,1,0:T(8,128)(2,1)S(1)} %bitcast.9), channel_id=1, source_target_pairs={{0,1},{1,0},{2,3},{3,2},{4,5},{5,4},{6,7},{7,6},{8,9},{9,8},{10,11... | collective-permute-start | bytes 393224 | tf_op jit(solution)/shard_map/ppermute | solution.py:87
  24.2 1.5 %collective-permute-start.11 = (bf16[1,128,256]{2,1,0:T(8,128)(2,1)S(1)}, bf16[1,128,256]{2,1,0:T(8,128)(2,1)S(1)}, u32[]{:S(2)}, u32[]{:S(2)}) collective-permute-start(bf16[1,128,256]{2,1,0:T(8,128)(2,1)S(1)} %slice.11.refs_4_), channel_id=1, source_target_pairs={{0,16},{4,20},{8,24},{12,28},{16,0},{20,4},{24,8},{28,12},{1,17},{... | collective-permute-start | bytes 196616 | tf_op jit(solution)/shard_map/ppermute | solution.py:87
  25.7 1.6 %collective-permute-start.7 = (bf16[2,128,256]{2,1,0:T(8,128)(2,1)S(1)}, bf16[2,128,256]{2,1,0:T(8,128)(2,1)S(1)}, u32[]{:S(2)}, u32[]{:S(2)}) collective-permute-start(bf16[2,128,256]{2,1,0:T(8,128)(2,1)S(1)} %pad_maximum_fusion.4), channel_id=1, source_target_pairs={{0,8},{4,12},{8,0},{12,4},{16,24},{20,28},{24,16},{28,20},{1,9},{5... | collective-permute-start | bytes 393224 | tf_op jit(solution)/shard_map/ppermute | solution.py:87
  27.3 1.2 %collective-permute-done.11.refs_5_ = bf16[1,128,256]{2,1,0:T(8,128)(2,1)S(1)} collective-permute-done((bf16[1,128,256]{2,1,0:T(8,128)(2,1)S(1)}, bf16[1,128,256]{2,1,0:T(8,128)(2,1)S(1)}, u32[]{:S(2)}, u32[]{:S(2)}) %collective-permute-start.11) | collective-permute-done | bytes 65568 | tf_op jit(solution)/shard_map/ppermute | solution.py:87
  28.5 0.8 %collective-permute-done.9.refs_9_ = bf16[1,2,128,256]{3,2,1,0:T(8,128)(2,1)S(1)} collective-permute-done((bf16[1,2,128,256]{3,2,1,0:T(8,128)(2,1)S(1)}, bf16[1,2,128,256]{3,2,1,0:T(8,128)(2,1)S(1)}, u32[]{:S(2)}, u32[]{:S(2)}) %collective-permute-start.9) | collective-permute-done | bytes 131104 | tf_op jit(solution)/shard_map/ppermute | solution.py:87
  29.4 1.6 %collective-permute-start.13 = (bf16[2,128,256]{2,1,0:T(8,128)(2,1)S(1)}, bf16[2,128,256]{2,1,0:T(8,128)(2,1)S(1)}, u32[]{:S(2)}, u32[]{:S(2)}) collective-permute-start(bf16[2,128,256]{2,1,0:T(8,128)(2,1)S(1)} %pad_maximum_fusion.5), channel_id=1, source_target_pairs={{0,8},{4,12},{8,0},{12,4},{16,24},{20,28},{24,16},{28,20},{1,9},{5... | collective-permute-start | bytes 393224 | tf_op jit(solution)/shard_map/ppermute | solution.py:87
  31.0 0.2 collective-permute-start.12
  31.3 3.1 %collective-permute-done.13.refs_6_ = bf16[2,128,256]{2,1,0:T(8,128)(2,1)S(1)} collective-permute-done((bf16[2,128,256]{2,1,0:T(8,128)(2,1)S(1)}, bf16[2,128,256]{2,1,0:T(8,128)(2,1)S(1)}, u32[]{:S(2)}, u32[]{:S(2)}) %collective-permute-start.13) | collective-permute-done | bytes 131104 | tf_op jit(solution)/shard_map/ppermute | solution.py:87
  34.5 1.4 %collective-permute-done.12.block_ref = bf16[1,2,128,256]{3,2,1,0:T(8,128)(2,1)S(1)} collective-permute-done((bf16[1,2,128,256]{3,2,1,0:T(8,128)(2,1)S(1)}, bf16[1,2,128,256]{3,2,1,0:T(8,128)(2,1)S(1)}, u32[]{:S(2)}, u32[]{:S(2)}) %collective-permute-start.12) | collective-permute-done | bytes 131104 | tf_op jit(solution)/shard_map/ppermute | solution.py:87
  36.0 1.0 %purify_step.1 = (bf16[128,256]{1,0:T(8,128)(2,1)S(1)}, f32[128,256]{1,0:T(8,128)S(1)}) custom-call(s32[2]{0:T(128)S(1)} %pad_add_fusion.refs_0_, bf16[2,128,256]{2,1,0:T(8,128)(2,1)S(1)} %get-tuple-element.20.refs_1_, f32[2,128,256]{2,1,0:T(8,128)S(1)} %get-tuple-element.15.refs_2_.refs_1_, bf16[1024,256]{1,0:T(8,128)(2,1)S(1)} %get-tuple-element.21.refs_3_, ...), custom_call_target="tpu_custom_call" | custom-call | flops 6000000000 | tf_op jit(solution)/shard_map/purify_step/pallas_call | solution.py:174
  37.0 1.5 %last_step.1 = (bf16[128,256]{1,0:T(8,128)(2,1)}, bf16[128,256]{1,0:T(8,128)(2,1)}) custom-call(s32[2]{0:T(128)S(1)} %pad_add_fusion.refs_0_, f32[2,128,256]{2,1,0:T(8,128)S(1)} %get-tuple-element.15.refs_2_.refs_1_, bf16[128,256]{1,0:T(8,128)(2,1)S(1)} %get-tuple-element.25.refs_2_, f32[128,256]{1,0:T(8,128)S(1)} %get-tuple-element.26.refs_3_, ...), custom_call_target="tpu_custom_call" | custom-call | tf_op jit(solution)/shard_map/last_step/pallas_call | solution.py:174
  (21 shorter events, 0.8 us)
Async XLA Ops:
  1.6 10.5 %collective-permute-start = (bf16[1,2,128,256]{3,2,1,0:T(8,128)(2,1)S(1)}, bf16[1,2,128,256]{3,2,1,0:T(8,128)(2,1)S(1)}, u32[]{:S(2)}, u32[]{:S(2)}) collective-permute-start(bf16[1,2,128,256]{3,2,1,0:T(8,128)(2,1)S(1)} %bitcast.4), channel_id=1, source_target_pairs={{0,2},{1,3},{2,0},{3,1},{4,6},{5,7},{6,4},{7,5},{8,10},{9,11},{10,... | collective-permute-start | bytes 393224 | tf_op jit(solution)/shard_map/ppermute | solution.py:87
  5.7 6.6 %collective-permute-start.1 = (bf16[1,2,128,256]{3,2,1,0:T(8,128)(2,1)S(1)}, bf16[1,2,128,256]{3,2,1,0:T(8,128)(2,1)S(1)}, u32[]{:S(2)}, u32[]{:S(2)}) collective-permute-start(bf16[1,2,128,256]{3,2,1,0:T(8,128)(2,1)S(1)} %bitcast.5), channel_id=1, source_target_pairs={{0,1},{1,0},{2,3},{3,2},{4,5},{5,4},{6,7},{7,6},{8,9},{9,8},{10,11... | collective-permute-start | bytes 393224 | tf_op jit(solution)/shard_map/ppermute | solution.py:87
  7.3 4.3 %collective-permute-start.2 = (bf16[1,128,256]{2,1,0:T(8,128)(2,1)S(1)}, bf16[1,128,256]{2,1,0:T(8,128)(2,1)S(1)}, u32[]{:S(2)}, u32[]{:S(2)}) collective-permute-start(bf16[1,128,256]{2,1,0:T(8,128)(2,1)S(1)} %get-tuple-element.29.refs_3_), channel_id=1, source_target_pairs={{0,16},{4,20},{8,24},{12,28},{16,0},{20,4},{24,8},{28,12},{1,17},{... | collective-permute-start | bytes 196616 | tf_op jit(solution)/shard_map/ppermute | solution.py:87
  12.3 5.0 %collective-permute-start.3 = (bf16[2,128,256]{2,1,0:T(8,128)(2,1)S(1)}, bf16[2,128,256]{2,1,0:T(8,128)(2,1)S(1)}, u32[]{:S(2)}, u32[]{:S(2)}) collective-permute-start(bf16[2,128,256]{2,1,0:T(8,128)(2,1)S(1)} %pad_maximum_fusion.3), channel_id=1, source_target_pairs={{0,8},{4,12},{8,0},{12,4},{16,24},{20,28},{24,16},{28,20},{1,9},{5... | collective-permute-start | bytes 393224 | tf_op jit(solution)/shard_map/ppermute | solution.py:87
  13.9 5.0 %collective-permute-start.5 = (bf16[1,2,128,256]{3,2,1,0:T(8,128)(2,1)S(1)}, bf16[1,2,128,256]{3,2,1,0:T(8,128)(2,1)S(1)}, u32[]{:S(2)}, u32[]{:S(2)}) collective-permute-start(bf16[1,2,128,256]{3,2,1,0:T(8,128)(2,1)S(1)} %collective-permute-done.refs_8_.refs_9_), channel_id=1, source_target_pairs={{0,1},{1,0},{2,3},{3,2},{4,5},{5,4},{6,7},{7,6},{8,9},{9,8},{10,11... | collective-permute-start | bytes 393224 | tf_op jit(solution)/shard_map/ppermute | solution.py:87
  15.4 10.3 %collective-permute-start.6 = (bf16[1,128,256]{2,1,0:T(8,128)(2,1)S(1)}, bf16[1,128,256]{2,1,0:T(8,128)(2,1)S(1)}, u32[]{:S(2)}, u32[]{:S(2)}) collective-permute-start(bf16[1,128,256]{2,1,0:T(8,128)(2,1)S(1)} %get-tuple-element.22.refs_4_), channel_id=1, source_target_pairs={{0,16},{4,20},{8,24},{12,28},{16,0},{20,4},{24,8},{28,12},{1,17},{... | collective-permute-start | bytes 196616 | tf_op jit(solution)/shard_map/ppermute | solution.py:87
  17.4 1.6 %collective-permute-start.4 = (bf16[4,128,256]{2,1,0:T(8,128)(2,1)S(1)}, bf16[4,128,256]{2,1,0:T(8,128)(2,1)S(1)}, u32[]{:S(2)}, u32[]{:S(2)}) collective-permute-start(bf16[4,128,256]{2,1,0:T(8,128)(2,1)S(1)} %pad_maximum_fusion), channel_id=1, source_target_pairs={{0,4},{4,0},{8,12},{12,8},{16,20},{20,16},{24,28},{28,24},{1,5},{5... | collective-permute-start | bytes 786440 | tf_op jit(solution)/shard_map/ppermute | solution.py:87
  19.9 9.4 %collective-permute-start.9 = (bf16[1,2,128,256]{3,2,1,0:T(8,128)(2,1)S(1)}, bf16[1,2,128,256]{3,2,1,0:T(8,128)(2,1)S(1)}, u32[]{:S(2)}, u32[]{:S(2)}) collective-permute-start(bf16[1,2,128,256]{3,2,1,0:T(8,128)(2,1)S(1)} %bitcast.8), channel_id=1, source_target_pairs={{0,2},{1,3},{2,0},{3,1},{4,6},{5,7},{6,4},{7,5},{8,10},{9,11},{10,... | collective-permute-start | bytes 393224 | tf_op jit(solution)/shard_map/ppermute | solution.py:87
  22.1 7.3 %collective-permute-start.10 = (bf16[1,2,128,256]{3,2,1,0:T(8,128)(2,1)S(1)}, bf16[1,2,128,256]{3,2,1,0:T(8,128)(2,1)S(1)}, u32[]{:S(2)}, u32[]{:S(2)}) collective-permute-start(bf16[1,2,128,256]{3,2,1,0:T(8,128)(2,1)S(1)} %bitcast.9), channel_id=1, source_target_pairs={{0,1},{1,0},{2,3},{3,2},{4,5},{5,4},{6,7},{7,6},{8,9},{9,8},{10,11... | collective-permute-start | bytes 393224 | tf_op jit(solution)/shard_map/ppermute | solution.py:87
  24.2 4.3 %collective-permute-start.11 = (bf16[1,128,256]{2,1,0:T(8,128)(2,1)S(1)}, bf16[1,128,256]{2,1,0:T(8,128)(2,1)S(1)}, u32[]{:S(2)}, u32[]{:S(2)}) collective-permute-start(bf16[1,128,256]{2,1,0:T(8,128)(2,1)S(1)} %slice.11.refs_4_), channel_id=1, source_target_pairs={{0,16},{4,20},{8,24},{12,28},{16,0},{20,4},{24,8},{28,12},{1,17},{... | collective-permute-start | bytes 196616 | tf_op jit(solution)/shard_map/ppermute | solution.py:87
  25.7 5.5 %collective-permute-start.7 = (bf16[2,128,256]{2,1,0:T(8,128)(2,1)S(1)}, bf16[2,128,256]{2,1,0:T(8,128)(2,1)S(1)}, u32[]{:S(2)}, u32[]{:S(2)}) collective-permute-start(bf16[2,128,256]{2,1,0:T(8,128)(2,1)S(1)} %pad_maximum_fusion.4), channel_id=1, source_target_pairs={{0,8},{4,12},{8,0},{12,4},{16,24},{20,28},{24,16},{28,20},{1,9},{5... | collective-permute-start | bytes 393224 | tf_op jit(solution)/shard_map/ppermute | solution.py:87
  29.4 5.0 %collective-permute-start.13 = (bf16[2,128,256]{2,1,0:T(8,128)(2,1)S(1)}, bf16[2,128,256]{2,1,0:T(8,128)(2,1)S(1)}, u32[]{:S(2)}, u32[]{:S(2)}) collective-permute-start(bf16[2,128,256]{2,1,0:T(8,128)(2,1)S(1)} %pad_maximum_fusion.5), channel_id=1, source_target_pairs={{0,8},{4,12},{8,0},{12,4},{16,24},{20,28},{24,16},{28,20},{1,9},{5... | collective-permute-start | bytes 393224 | tf_op jit(solution)/shard_map/ppermute | solution.py:87
  31.0 5.0 %collective-permute-start.12 = (bf16[1,2,128,256]{3,2,1,0:T(8,128)(2,1)S(1)}, bf16[1,2,128,256]{3,2,1,0:T(8,128)(2,1)S(1)}, u32[]{:S(2)}, u32[]{:S(2)}) collective-permute-start(bf16[1,2,128,256]{3,2,1,0:T(8,128)(2,1)S(1)} %collective-permute-done.9.refs_9_), channel_id=1, source_target_pairs={{0,1},{1,0},{2,3},{3,2},{4,5},{5,4},{6,7},{7,6},{8,9},{9,8},{10,11... | collective-permute-start | bytes 393224 | tf_op jit(solution)/shard_map/ppermute | solution.py:87
  31.3 4.7 %collective-permute-start.8 = (bf16[4,128,256]{2,1,0:T(8,128)(2,1)S(1)}, bf16[4,128,256]{2,1,0:T(8,128)(2,1)S(1)}, u32[]{:S(2)}, u32[]{:S(2)}) collective-permute-start(bf16[4,128,256]{2,1,0:T(8,128)(2,1)S(1)} %pad_maximum_fusion.1), channel_id=1, source_target_pairs={{0,4},{4,0},{8,12},{12,8},{16,20},{20,16},{24,28},{28,24},{1,5},{5... | collective-permute-start | bytes 786440 | tf_op jit(solution)/shard_map/ppermute | solution.py:87
  34.5 2.5 %collective-permute-start.14 = (bf16[4,128,256]{2,1,0:T(8,128)(2,1)S(1)}, bf16[4,128,256]{2,1,0:T(8,128)(2,1)S(1)}, u32[]{:S(2)}, u32[]{:S(2)}) collective-permute-start(bf16[4,128,256]{2,1,0:T(8,128)(2,1)S(1)} %pad_maximum_fusion.2), channel_id=1, source_target_pairs={{0,4},{4,0},{8,12},{12,8},{16,20},{20,16},{24,28},{28,24},{1,5},{5... | collective-permute-start | bytes 786440 | tf_op jit(solution)/shard_map/ppermute | solution.py:87
